TPU v7x, 32 devices: a whole 2x2x4 slice. The times are simulated.
32 devices in a mesh: ens: 2 (over y), mom: 8 (over z, x), src: 2 (over core).
Axes of the slice: x: 2, y: 2, z: 4, core: 2. Of those that a mesh axis runs over, the one named last changes fastest.
Arguments:
- fields: bfloat16 [16, 8, 2, 6, 2, 128, 128], P(('ens', 'mom'), 'src'), parts along dimension 0, may hold values from -0.29882812 to 0.29882812
- block_cols: int32 [16, 8, 6, 2], P(('ens', 'mom'), 'src'), parts along dimension 0, may hold values from 0 to 5, as said below
- sources: int32 [2], P('src'), may hold values from 0 to 7, as said below
- deltas: int32 [4], replicated, may hold values from 1 to 7
- partner: int32 [8], P('mom'), may hold values from 0 to 7, as said below
Outputs:
- correlator: float32 [2, 4, 16], P(None, 'src', ('ens', 'mom')), parts along dimension 2
There are 2 independent parts, one for each index of `ens`. A program takes and returns all parts, laid end to end along the dimension named above; an argument that names none is the same for every part. Nothing has to cross between parts.
Inputs may be any that keep to these rules, and one draw needn't show every extreme that they name: `block_cols`: within each block row of each field the 2 block columns are distinct. `sources`: entry s lies among the timeslices s * 4 to (s + 1) * 4 - 1. partner is an involution without fixed points. Momenta g * 1 to (g + 1) - 1 form group g; the partners of group g's momenta are the momenta of group g XOR (8 / 2).
All inputs are finite; a program needn't handle non-finite values.
Results may differ from a plain program's by a relative error of at most 0.0095.
Values may be sent and summed in bfloat16 or wider, within the bound.
No kernel may reach another device: no remote copies, remote signals or barrier semaphores. Data moves between devices by JAX's collectives and lax.ppermute only.
A program may use at most 128 MiB of HBM per device.

v0:
```python
import jax
import jax.numpy as jnp
from jax import lax
from jax.experimental import pallas as pl
from jax.experimental.pallas import tpu as pltpu
from jax.sharding import PartitionSpec as P

F32 = jnp.float32
BF16 = jnp.bfloat16
I32 = jnp.int32
SMEM = pl.BlockSpec(memory_space=pltpu.SMEM)
VMEM = pl.BlockSpec(memory_space=pltpu.VMEM)
ANY = pl.BlockSpec(memory_space=pl.ANY)


def one_way_pairs(count):
    half = count // 2
    outer = half // 2
    return [(g + half, g) if g < outer else (g, g + half) for g in range(half)]


def cost(flops, size):
    return pl.CostEstimate(flops=flops, bytes_accessed=size, transcendentals=0)


def pick_source_kernel(source_ref, fields_ref, out_ref, sems):
    time = lax.rem(source_ref[0], I32(fields_ref.shape[0]))
    copies = [
        pltpu.make_async_copy(fields_ref.at[time, part, r], out_ref.at[part, r], sems.at[part, r])
        for part in range(fields_ref.shape[1])
        for r in range(fields_ref.shape[2])
    ]
    for copy in copies:
        copy.start()
    for copy in copies:
        copy.wait()


def pick_source(source, fields):
    return pl.pallas_call(
        pick_source_kernel,
        out_shape=jax.ShapeDtypeStruct(fields.shape[1:], fields.dtype),
        in_specs=[SMEM, ANY],
        out_specs=VMEM,
        scratch_shapes=[pltpu.SemaphoreType.DMA(fields.shape[1:3])],
        cost_estimate=cost(0, 1_600_000),
        compiler_params=pltpu.CompilerParams(vmem_limit_bytes=52 * 2**20),
        name="pick_source",
    )(source, fields)


def pick_kernel(order_ref, fields_ref, *refs):
    *outs, sems = refs
    copies = [
        pltpu.make_async_copy(fields_ref.at[order_ref[slot + 1], part], out.at[part], sems.at[slot, part])
        for slot, out in enumerate(outs)
        for part in range(2)
    ]
    for copy in copies:
        copy.start()
    for copy in copies:
        copy.wait()


def pick_others(order, fields):
    others = fields.shape[0] - 1
    return pl.pallas_call(
        pick_kernel,
        out_shape=[jax.ShapeDtypeStruct(fields.shape[1:], fields.dtype)] * others,
        in_specs=[SMEM, ANY],
        out_specs=[VMEM] * others,
        scratch_shapes=[pltpu.SemaphoreType.DMA((others, 2))],
        cost_estimate=cost(0, others * 1_600_000),
        compiler_params=pltpu.CompilerParams(vmem_limit_bytes=58 * 2**20),
        name="pick_others",
    )(order, fields)


def plan_kernel(core_ref, own_ref, other_ref, deltas_ref, order_ref, sinks_ref, active_ref, full_ref):
    times = order_ref.shape[0]
    deltas = deltas_ref.shape[0]
    sinks = []
    for s, ref in enumerate((own_ref, other_ref)):
        for k in range(deltas):
            sink = lax.rem(ref[0] + deltas_ref[k], I32(2 * times))
            sinks_ref[s * deltas + k] = sink
            sinks.append(sink)
    base = core_ref[0] * times
    first = own_ref[0] - base
    keys = []
    for t in range(times):
        needed = sinks[0] == base + t
        for sink in sinks[1:]:
            needed = needed | (sink == base + t)
        key = jnp.where(needed, I32(t), I32(times + t))
        keys.append(jnp.where(first == t, I32(-1), key))
    for t in range(times):
        rank = I32(0)
        for other in range(times):
            if other != t:
                rank += (keys[other] < keys[t]).astype(I32)
        order_ref[rank] = I32(t)
        for s in range(2):
            active = sinks[s * deltas] == base + t
            for k in range(1, deltas):
                active = active | (sinks[s * deltas + k] == base + t)
            active_ref[s * times + rank] = active.astype(I32)
    full = I32(0)
    for c in range(2):
        count = I32(0)
        for t in range(times):
            needed = (own_ref[0] == c * times + t) | (other_ref[0] == c * times + t)
            for sink in sinks:
                needed = needed | (sink == c * times + t)
            count += needed.astype(I32)
        full += jnp.where(count == times, I32(1 << c), I32(0))
    full_ref[0] = full


def plan(core, own, other, deltas, times):
    return pl.pallas_call(
        plan_kernel,
        out_shape=[
            jax.ShapeDtypeStruct((times,), I32),
            jax.ShapeDtypeStruct((2 * deltas.shape[0],), I32),
            jax.ShapeDtypeStruct((2 * times,), I32),
            jax.ShapeDtypeStruct((1,), I32),
        ],
        in_specs=[SMEM] * 4,
        out_specs=[SMEM] * 4,
        cost_estimate=cost(0, 1000),
        name="plan",
    )(core, own, other, deltas)


def weights_kernel(s, order_ref, active_ref, *refs):
    far_ref, own_ref, far_cols, own_cols, m_cols, b_cols, a_ref, d_ref, *refs = refs
    *b_refs, u_ref, la, ld, bs, yn, held, sems = refs
    slot = pl.program_id(0)
    rows, per_row, size = a_ref.shape[1], a_ref.shape[2], a_ref.shape[3]
    times = order_ref.shape[0]
    step = rows * per_row
    base = order_ref[slot] * step
    a_base = lax.rem(far_ref[0], I32(times)) * step
    d_base = lax.rem(own_ref[0], I32(times)) * step
    lo, hi = pl.ds(0, size), pl.ds(size, size)

    b_copies = [
        pltpu.make_async_copy(b_ref, held.at[at % 2], sems.at[at % 2]) for at, b_ref in enumerate(b_refs)
    ]

    @pl.when(slot == 0)
    def _():
        b_copies[0].start()
        for r in range(rows):
            for j in range(per_row):
                real, imag = a_ref[0, r, j], a_ref[1, r, j]
                la[r, j, lo, lo] = real
                la[r, j, lo, hi] = -imag
                la[r, j, hi, lo] = imag
                la[r, j, hi, hi] = real
                real, imag = d_ref[0, r, j].T, d_ref[1, r, j].T
                ld[r, j, lo, lo] = real
                ld[r, j, lo, hi] = -imag
                ld[r, j, hi, lo] = imag
                ld[r, j, hi, hi] = real

    for at in range(times):

        @pl.when(slot == at)
        def _():
            if at + 1 < times:
                b_copies[at + 1].start()
            b_copies[at].wait()

    @pl.when(active_ref[s * times + slot] == 0)
    def _():
        u_ref[...] = jnp.zeros_like(u_ref)

    @pl.when(active_ref[s * times + slot] != 0)
    def _():
        for r in range(rows):
            for j in range(per_row):
                bs[r, lo, pl.ds(j * size, size)] = held[slot % 2, 0, r, j]
                bs[r, hi, pl.ds(j * size, size)] = held[slot % 2, 1, r, j]

        yn[...] = jnp.zeros_like(yn)
        for r in range(rows):
            inners = [far_cols[a_base + r * per_row + j] for j in range(per_row)]
            parts = [
                jnp.dot(la[r, j], bs[inners[j]], preferred_element_type=F32) for j in range(per_row)
            ]
            pieces = []
            for j in range(per_row):
                for k in range(per_row):
                    col = b_cols[base + inners[j] * per_row + k]
                    pieces.append((j, col, parts[j][:, k * size : (k + 1) * size]))
            for at in reversed(range(len(pieces))):
                j, col, value = pieces[at]
                for other_j, other_col, other in pieces:
                    if other_j > j:
                        value = value + jnp.where(other_col == col, 1.0, 0.0) * other
                yn[col, pl.ds(r * size, size), lo] = value[:size].astype(BF16)
                yn[col, pl.ds(r * size, size), hi] = value[size:].astype(BF16)

        trace_real = jnp.zeros((size, size), F32)
        trace_imag = jnp.zeros((size, size), F32)
        for r in range(rows):
            trace_real += yn[r, pl.ds(r * size, size), lo].astype(F32)
            trace_imag += yn[r, pl.ds(r * size, size), hi].astype(F32)
        diagonal = lax.broadcasted_iota(I32, (size, size), 0) == lax.broadcasted_iota(I32, (size, size), 1)
        trace_real = jnp.sum(jnp.where(diagonal, trace_real, 0.0))
        trace_imag = jnp.sum(jnp.where(diagonal, trace_imag, 0.0))

        for r in range(rows):
            for j in range(per_row):
                col = m_cols[base + r * per_row + j]
                pick = I32(0)
                keep = F32(0)
                for k in range(per_row):
                    hit = own_cols[d_base + col * per_row + k] == r
                    pick = jnp.where(hit, I32(k), pick)
                    keep = jnp.where(hit, F32(1), keep)
                real = ld[col, pick, lo, lo].astype(F32)
                imag = ld[col, pick, hi, lo].astype(F32)
                weight_real, weight_imag = trace_real * keep, trace_imag * keep
                u_ref[0, r, j, 0] = weight_real * real - weight_imag * imag
                u_ref[0, r, j, 1] = weight_real * imag + weight_imag * real

        for i in range(rows):
            for j in range(per_row):
                r = own_cols[d_base + i * per_row + j]
                met = [m_cols[base + r * per_row + k] for k in range(per_row)]
                right = jnp.concatenate(
                    [yn[i, pl.ds(pl.multiple_of(col * size, size), size)] for col in met], axis=0
                )
                part = lax.dot_general(
                    ld[i, j], right, (((1,), (1,)), ((), ())), preferred_element_type=F32
                )
                for k in range(per_row):
                    u_ref[0, r, k, 0] -= part[:size, k * size : (k + 1) * size]
                    u_ref[0, r, k, 1] -= part[size:, k * size : (k + 1) * size]


def weights(flops, s, order, active, far_time, own_time, far_cols, own_cols, m_cols, b_cols, a, d, picked):
    times = len(picked)
    _, rows, per_row, size, _ = a.shape
    whole = lambda slot, *_: (0, 0, 0, 0, 0)
    return pl.pallas_call(
        lambda *refs: weights_kernel(s, *refs),
        out_shape=jax.ShapeDtypeStruct((times, rows, per_row, 2, size, size), F32),
        grid_spec=pltpu.PrefetchScalarGridSpec(
            num_scalar_prefetch=8,
            grid=(times,),
            in_specs=[
                pl.BlockSpec(a.shape, whole),
                pl.BlockSpec(a.shape, whole),
                *[ANY] * times,
            ],
            out_specs=pl.BlockSpec(
                (1, rows, per_row, 2, size, size), lambda slot, *_: (slot, 0, 0, 0, 0, 0)
            ),
            scratch_shapes=[
                pltpu.VMEM((rows, per_row, 2 * size, 2 * size), BF16),
                pltpu.VMEM((rows, per_row, 2 * size, 2 * size), BF16),
                pltpu.VMEM((rows, 2 * size, per_row * size), BF16),
                pltpu.VMEM((rows, rows * size, 2 * size), BF16),
                pltpu.VMEM((2,) + a.shape, a.dtype),
                pltpu.SemaphoreType.DMA((2,)),
            ],
        ),
        compiler_params=pltpu.CompilerParams(vmem_limit_bytes=24 * 2**20),
        cost_estimate=cost(flops, times * 1_000_000),
        name="weights",
    )(order, active, far_time, own_time, far_cols, own_cols, m_cols, b_cols, a, d, *picked)


def products(field_ref, u_refs, slot, held, sems):
    _, rows, per_row, size, _ = field_ref.shape
    copies = [
        [
            pltpu.make_async_copy(field_ref.at[part, r], held.at[part, r], sems.at[part, r])
            for part in range(2)
        ]
        for r in range(rows)
    ]
    for row in copies:
        for copy in row:
            copy.start()
    chunk = min(size, 32)
    fold = lambda x: jnp.sum(x.reshape(chunk // 8, 8, size), axis=0)
    sums = [jnp.zeros((8, size), F32) for _ in range(2 * len(u_refs))]
    for r in range(rows):
        for copy in copies[r]:
            copy.wait()
        for j in range(per_row):
            for start in range(0, size, chunk):
                at = pl.ds(start, chunk)
                real = held[0, r, j, at].astype(F32)
                imag = held[1, r, j, at].astype(F32)
                for s, u_ref in enumerate(u_refs):
                    u_real, u_imag = u_ref[slot, r, j, 0, at], u_ref[slot, r, j, 1, at]
                    sums[2 * s] += fold(real * u_real - imag * u_imag)
                    sums[2 * s + 1] += fold(real * u_imag + imag * u_real)
    return sums


def products_scratch(field):
    return [pltpu.VMEM(field.shape, field.dtype), pltpu.SemaphoreType.DMA(field.shape[:2])]


def inner_kernel(slot, field_ref, u0_ref, u1_ref, out_ref, held, sems):
    for at, value in enumerate(products(field_ref, (u0_ref, u1_ref), slot, held, sems)):
        out_ref[at] = value


def inner(slot, field, u0, u1):
    return pl.pallas_call(
        lambda *refs: inner_kernel(slot, *refs),
        out_shape=jax.ShapeDtypeStruct((4, 8, field.shape[-1]), F32),
        in_specs=[ANY, VMEM, VMEM],
        out_specs=VMEM,
        scratch_shapes=products_scratch(field),
        cost_estimate=cost(4_000_000, 4_000_000),
        compiler_params=pltpu.CompilerParams(vmem_limit_bytes=24 * 2**20),
        name="inner",
    )(field, u0, u1)


def stage_kernel(slot, u0_ref, u1_ref, out0_ref, out1_ref, sems):
    copies = [
        pltpu.make_async_copy(u_ref.at[slot, r], out_ref.at[0, r], sems.at[s, r])
        for s, (u_ref, out_ref) in enumerate(((u0_ref, out0_ref), (u1_ref, out1_ref)))
        for r in range(u_ref.shape[1])
    ]
    for copy in copies:
        copy.start()
    for copy in copies:
        copy.wait()


def stage(slot, u0, u1):
    one = jax.ShapeDtypeStruct((1,) + u0.shape[1:], u0.dtype)
    return pl.pallas_call(
        lambda *refs: stage_kernel(slot, *refs),
        out_shape=[one, one],
        in_specs=[ANY] * 2,
        out_specs=[VMEM] * 2,
        scratch_shapes=[pltpu.SemaphoreType.DMA((2, u0.shape[1]))],
        cost_estimate=cost(0, 6_000_000),
        compiler_params=pltpu.CompilerParams(vmem_limit_bytes=24 * 2**20),
        name="stage",
    )(u0, u1)


def last_kernel(core_ref, order_ref, sinks_ref, *refs):
    *others, field_ref, u0_ref, u1_ref, mine_ref, theirs_ref, held, sems = refs
    slots = order_ref.shape[0]
    deltas = sinks_ref.shape[0] // 2
    share = deltas // 2
    core = core_ref[0]
    sums = [[ref[at] for at in range(4)] for ref in others]
    sums.insert(slots - 2, products(field_ref, (u0_ref, u1_ref), 0, held, sems))
    for out_ref, owner in ((mine_ref, core), (theirs_ref, 1 - core)):
        lines = [jnp.zeros(sums[0][0].shape, F32) for _ in range(2 * share)]
        for slot in range(slots):
            time = core * slots + order_ref[slot]
            for s in range(2):
                for k in range(share):
                    sink = sinks_ref[s * deltas + owner * share + k]
                    keep = jnp.where(sink == time, F32(1), F32(0))
                    for part in range(2):
                        lines[part * share + k] += keep * sums[slot][2 * s + part]
        table = jnp.concatenate([jnp.sum(line, axis=0, keepdims=True) for line in lines], axis=0)
        table = jnp.sum(table, axis=1, keepdims=True)
        for part in range(2):
            out_ref[part] = table[part * share : (part + 1) * share]


def last(core, order, sinks, others, field, u0, u1):
    share = sinks.shape[0] // 4
    return pl.pallas_call(
        last_kernel,
        out_shape=[jax.ShapeDtypeStruct((2, share, 1), F32)] * 2,
        in_specs=[SMEM] * 3 + [VMEM] * len(others) + [ANY, VMEM, VMEM],
        out_specs=[VMEM] * 2,
        scratch_shapes=products_scratch(field),
        cost_estimate=cost(4_000_000, 4_000_000),
        compiler_params=pltpu.CompilerParams(vmem_limit_bytes=24 * 2**20),
        name="last",
    )(core, order, sinks, *others, field, u0, u1)


def local(fields, block_cols, sources, deltas, partner):
    assert fields.shape[0] == 1 and lax.axis_size("src") == 2
    del partner
    fields = fields[0]
    times = fields.shape[0]
    core = lax.axis_index("src").reshape(1)
    pairs = one_way_pairs(lax.axis_size("mom"))
    swap = lambda value: lax.ppermute(value, "src", [(0, 1), (1, 0)])
    to_partner = lambda value: lax.ppermute(value, "mom", pairs)

    cols = block_cols.reshape(-1)
    far_cols = to_partner(cols)
    own_field = pick_source(sources, fields)
    far = [to_partner(own_field)]

    other_time = swap(sources)
    order, sinks, active, full = plan(core, sources, other_time, deltas, times)
    others = pick_others(order, fields)
    picked = [own_field, *others]
    *early, late = others
    for field in early:
        if len(far) > 1:
            field, far[-2] = lax.optimization_barrier((field, far[-2]))
        far.append(to_partner(field))

    other_cols = swap(cols)
    far_other_cols = swap(far_cols)
    other_field = swap(own_field)
    far_other = swap(far[0])
    u0 = weights(
        80_000_000_000,
        0,
        order,
        active,
        sources,
        sources,
        far_cols,
        cols,
        far_cols,
        cols,
        far[0],
        own_field,
        picked,
    )
    u1 = weights(
        2_000_000_000,
        1,
        order,
        active,
        other_time,
        other_time,
        far_other_cols,
        other_cols,
        far_cols,
        cols,
        far_other,
        other_field,
        picked,
    )
    sums = [inner(slot, far[slot], u0, u1) for slot in range(times - 2)]

    both = ("mom", "src")

    def with_slot(cores):
        routes = [(2 * a + c, 2 * b + c) for a, b in pairs for c in cores]

        def branch(field, u0, u1):
            field = lax.ppermute(field, both, routes)
            return inner(times - 1, field, u0, u1), *stage(times - 2, u0, u1)

        return branch

    def without_slot(field, u0, u1):
        return jnp.zeros(sums[0].shape, F32), *stage(times - 2, u0, u1)

    branches = [without_slot, with_slot([0]), with_slot([1]), with_slot([0, 1])]
    late, *sums = lax.optimization_barrier((late, *sums))
    late_sums, staged0, staged1 = lax.switch(full[0], branches, late, u0, u1)
    mine, theirs = last(core, order, sinks, [*sums, late_sums], far[-1], staged0, staged1)

    total = mine + swap(theirs)
    back = [(2 * a + c, 2 * b + c) for b, a in pairs for c in range(2)]
    return total + lax.ppermute(total, both, back)


def solution(mesh):
    in_specs = (
        P(("ens", "mom"), "src", None, None, None, None, None),
        P(("ens", "mom"), "src", None, None),
        P("src"),
        P(),
        P("mom"),
    )
    out_specs = P(None, "src", ("ens", "mom"))
    return jax.shard_map(local, mesh=mesh, in_specs=in_specs, out_specs=out_specs, check_vma=False)
```

profile of v0, /device:TPU:8, one launch (start us, length us, event | category | flops | bytes accessed | tf_op | source)
XLA Modules:
  0.0 67.4 jit_solution(625852610010649191)
XLA Ops:
  0.7 0.0 copy-start.6
  0.7 1.3 %pick_source.1.refs_9_.refs_10_ = bf16[2,6,2,128,128]{4,3,2,1,0:T(8,128)(2,1)S(1)} custom-call(s32[1]{0:T(128)S(6)} %copy.21.own_ref.source_ref.refs_2_.refs_3_, bf16[4,2,6,2,128,128]{5,4,3,2,1,0:T(8,128)(2,1)} %bitcast.3), custom_call_target="tpu_custom_call" | custom-call | bytes 1600000 | tf_op jit(solution)/shard_map/pick_source/pallas_call | solution.py:40
  1.9 4.5 %collective-permute-start.4 = (bf16[2,6,2,128,128]{4,3,2,1,0:T(8,128)(2,1)S(1)}, bf16[2,6,2,128,128]{4,3,2,1,0:T(8,128)(2,1)S(1)}, u32[]{:S(2)}, u32[]{:S(2)}) collective-permute-start(bf16[2,6,2,128,128]{4,3,2,1,0:T(8,128)(2,1)S(1)} %pick_source.1.refs_9_.refs_10_), channel_id=1, source_target_pairs={{8,0},{10,2},{4,12},{6,14},{9,1},{11,3},{5,13},{7,15},{24,16},{26,... | collective-permute-start | bytes 2359304 | tf_op jit(solution)/shard_map/ppermute | solution.py:402
  6.5 0.1 collective-permute-start.3
  6.6 0.0 copy-done.6
  6.6 0.1 copy.7
  6.7 0.1 reshape.10.refs_5_.refs_7_
  6.8 0.6 collective-permute-start.7
  7.3 1.3 %collective-permute-start.5 = (s32[48]{0:T(128)S(1)}, s32[48]{0:T(128)S(1)}, u32[]{:S(2)}, u32[]{:S(2)}) collective-permute-start(s32[48]{0:T(128)S(1)} %reshape.10.refs_5_.refs_7_), channel_id=1, source_target_pairs={{8,0},{10,2},{4,12},{6,14},{9,1},{11,3},{5,13},{7,15},{24,16},{26,... | collective-permute-start | bytes 584 | tf_op jit(solution)/shard_map/ppermute | solution.py:402
  8.6 0.1 collective-permute-start.9
  8.7 0.0 collective-permute-done.3.other_ref.refs_2_.refs_3_
  8.7 1.9 %plan.1 = (s32[4]{0:T(128)}, s32[8]{0:T(128)}, s32[8]{0:T(128)}, s32[1]{0:T(128)}) custom-call(s32[1]{0:T(128)} %bitcast.core_ref, s32[1]{0:T(128)S(6)} %copy.21.own_ref.source_ref.refs_2_.refs_3_, s32[1]{0:T(128)} %collective-permute-done.3.other_ref.refs_2_.refs_3_, s32[4]{0:T(128)} %deltas_ref.1), custom_call_target="tpu_custom_call" | custom-call | bytes 1000 | tf_op jit(solution)/shard_map/plan/pallas_call | solution.py:121
  10.7 0.0 copy-start.3
  10.7 0.0 copy-start.5
  10.7 3.5 %pick_others.1 = (bf16[2,6,2,128,128]{4,3,2,1,0:T(8,128)(2,1)}, bf16[2,6,2,128,128]{4,3,2,1,0:T(8,128)(2,1)}, bf16[2,6,2,128,128]{4,3,2,1,0:T(8,128)(2,1)S(1)}) custom-call(s32[4]{0:T(128)} %get-tuple-element.63.order_ref.refs_0_, bf16[4,2,6,2,128,128]{5,4,3,2,1,0:T(8,128)(2,1)} %bitcast.4), custom_call_target="tpu_custom_call" | custom-call | bytes 4800000 | tf_op jit(solution)/shard_map/pick_others/pallas_call | solution.py:67
  14.2 1.3 %collective-permute-start.10 = (bf16[2,6,2,128,128]{4,3,2,1,0:T(8,128)(2,1)}, bf16[2,6,2,128,128]{4,3,2,1,0:T(8,128)(2,1)S(1)}, u32[]{:S(2)}, u32[]{:S(2)}) collective-permute-start(bf16[2,6,2,128,128]{4,3,2,1,0:T(8,128)(2,1)} %get-tuple-element.69.refs_11_), channel_id=1, source_target_pairs={{8,0},{10,2},{4,12},{6,14},{9,1},{11,3},{5,13},{7,15},{24,16},{26,... | collective-permute-start | bytes 2359304 | tf_op jit(solution)/shard_map/ppermute | solution.py:402
  16.1 8.3 %collective-permute-done.5.refs_4_.refs_6_ = s32[48]{0:T(128)S(1)} collective-permute-done((s32[48]{0:T(128)S(1)}, s32[48]{0:T(128)S(1)}, u32[]{:S(2)}, u32[]{:S(2)}) %collective-permute-start.5) | collective-permute-done | bytes 224 | tf_op jit(solution)/shard_map/ppermute | solution.py:402
  24.4 0.0 collective-permute-start.6
  24.4 0.0 collective-permute-done.4.refs_8_.refs_0_
  24.4 6.2 %collective-permute-start.11 = (bf16[2,6,2,128,128]{4,3,2,1,0:T(8,128)(2,1)}, bf16[2,6,2,128,128]{4,3,2,1,0:T(8,128)(2,1)}, u32[]{:S(2)}, u32[]{:S(2)}) collective-permute-start(bf16[2,6,2,128,128]{4,3,2,1,0:T(8,128)(2,1)} %get-tuple-element.75.refs_12_), channel_id=1, source_target_pairs={{8,0},{10,2},{4,12},{6,14},{9,1},{11,3},{5,13},{7,15},{24,16},{26,... | collective-permute-start | bytes 2359304 | tf_op jit(solution)/shard_map/ppermute | solution.py:402
  30.6 0.0 collective-permute-done.7.refs_5_
  30.6 0.2 collective-permute-start.8
  30.9 0.0 copy-done.3
  30.9 0.0 copy-done.5
  30.9 0.0 copy-start
  30.9 1.1 %copy-done = bf16[2,6,2,128,128]{4,3,2,1,0:T(8,128)(2,1)S(1)} copy-done((bf16[2,6,2,128,128]{4,3,2,1,0:T(8,128)(2,1)S(1)}, bf16[2,6,2,128,128]{4,3,2,1,0:T(8,128)(2,1)}, u32[]{:S(2)}) %copy-start) | copy-done | bytes 786456
  32.0 0.0 copy-start.2
  32.0 1.1 %copy-done.2 = bf16[2,6,2,128,128]{4,3,2,1,0:T(8,128)(2,1)S(1)} copy-done((bf16[2,6,2,128,128]{4,3,2,1,0:T(8,128)(2,1)S(1)}, bf16[2,6,2,128,128]{4,3,2,1,0:T(8,128)(2,1)}, u32[]{:S(2)}) %copy-start.2) | copy-done | bytes 786456
  33.1 5.5 %weights.2.refs_1_ = f32[4,6,2,2,128,128]{5,4,3,2,1,0:T(8,128)S(1)} custom-call(s32[4]{0:T(128)S(1)} %copy-done.3, s32[8]{0:T(128)S(1)} %copy-done.5, s32[1]{0:T(128)S(6)} %copy.21.own_ref.source_ref.refs_2_.refs_3_, s32[1]{0:T(128)S(6)} %copy.21.own_ref.source_ref.refs_2_.refs_3_, s32[48]{0:T(128)S(1)} %collective-permute-done.5.refs_4_.refs_6_, ...), custom_call_target="tpu_custom_call" | custom-call | flops 80000000000 | bytes 4000000 | tf_op jit(solution)/shard_map/weights/pallas_call | solution.py:249
  38.6 0.0 collective-permute-done.6.refs_4_
  38.6 0.0 collective-permute-done.9.refs_9_
  38.6 0.0 collective-permute-done.8.refs_8_
  38.7 0.0 copy-done.1
  38.7 6.7 %weights.3.refs_2_ = f32[4,6,2,2,128,128]{5,4,3,2,1,0:T(8,128)S(1)} custom-call(s32[4]{0:T(128)S(1)} %copy-done.3, s32[8]{0:T(128)S(1)} %copy-done.5, s32[1]{0:T(128)} %collective-permute-done.3.other_ref.refs_2_.refs_3_, s32[1]{0:T(128)} %collective-permute-done.3.other_ref.refs_2_.refs_3_, s32[48]{0:T(128)S(1)} %collective-permute-done.6.refs_4_, ...), custom_call_target="tpu_custom_call" | custom-call | flops 2000000000 | bytes 4000000 | tf_op jit(solution)/shard_map/weights/pallas_call | solution.py:249
  45.4 1.7 %inner.8.refs_0_ = f32[4,8,128]{2,1,0:T(8,128)S(1)} custom-call(bf16[2,6,2,128,128]{4,3,2,1,0:T(8,128)(2,1)S(1)} %collective-permute-done.4.refs_8_.refs_0_, f32[4,6,2,2,128,128]{5,4,3,2,1,0:T(8,128)S(1)} %weights.2.refs_1_, f32[4,6,2,2,128,128]{5,4,3,2,1,0:T(8,128)S(1)} %weights.3.refs_2_), custom_call_target="tpu_custom_call" | custom-call | flops 4000000 | bytes 4000000 | tf_op jit(solution)/shard_map/inner/pallas_call | solution.py:318
  47.1 0.0 collective-permute-done.10.refs_0_
  47.1 1.7 %inner.9.refs_1_ = f32[4,8,128]{2,1,0:T(8,128)S(1)} custom-call(bf16[2,6,2,128,128]{4,3,2,1,0:T(8,128)(2,1)S(1)} %collective-permute-done.10.refs_0_, f32[4,6,2,2,128,128]{5,4,3,2,1,0:T(8,128)S(1)} %weights.2.refs_1_, f32[4,6,2,2,128,128]{5,4,3,2,1,0:T(8,128)S(1)} %weights.3.refs_2_), custom_call_target="tpu_custom_call" | custom-call | flops 4000000 | bytes 4000000 | tf_op jit(solution)/shard_map/inner/pallas_call | solution.py:318
  48.7 0.0 copy-start.4
  48.7 0.4 conditional.1
  48.8 0.3 stage.4
  49.2 7.9 %collective-permute-done.11.refs_3_ = bf16[2,6,2,128,128]{4,3,2,1,0:T(8,128)(2,1)} collective-permute-done((bf16[2,6,2,128,128]{4,3,2,1,0:T(8,128)(2,1)}, bf16[2,6,2,128,128]{4,3,2,1,0:T(8,128)(2,1)}, u32[]{:S(2)}, u32[]{:S(2)}) %collective-permute-start.11) | collective-permute-done | bytes 786464 | tf_op jit(solution)/shard_map/ppermute | solution.py:402
  57.0 0.0 copy-done.4
  57.0 2.1 %last.1 = (f32[2,2,1]{2,1,0:T(2,128)S(1)}, f32[2,2,1]{2,1,0:T(2,128)S(1)}) custom-call(s32[1]{0:T(128)} %bitcast.core_ref, s32[4]{0:T(128)S(1)} %copy-done.3, s32[8]{0:T(128)S(1)} %copy-done.4, f32[4,8,128]{2,1,0:T(8,128)S(1)} %inner.8.refs_0_, f32[4,8,128]{2,1,0:T(8,128)S(1)} %inner.9.refs_1_, f32[4,8,128]{2,1,0:T(8,128)S(1)} %get-tuple-element.74.refs_2_, ...), custom_call_target="tpu_custom_call" | custom-call | flops 4000000 | bytes 4000000 | tf_op jit(solution)/shard_map/last/pallas_call | solution.py:382
  59.2 0.1 collective-permute-start.12
  59.3 1.1 %collective-permute-done.12 = f32[2,2,1]{2,1,0:T(2,128)S(1)} collective-permute-done((f32[2,2,1]{2,1,0:T(2,128)S(1)}, f32[2,2,1]{2,1,0:T(2,128)S(1)}, u32[]{:S(2)}, u32[]{:S(2)}) %collective-permute-start.12) | collective-permute-done | bytes 48 | tf_op jit(solution)/shard_map/ppermute | solution.py:401
  60.4 1.3 %collective-permute-start.13 = (f32[2,2,1]{2,1,0:T(2,128)S(1)}, f32[2,2,1]{2,1,0:T(2,128)S(1)}, u32[]{:S(2)}, u32[]{:S(2)}) collective-permute-start(f32[2,2,1]{2,1,0:T(2,128)S(1)} %add.6), channel_id=1, source_target_pairs={{0,8},{1,9},{2,10},{3,11},{12,4},{13,5},{14,6},{15,7},{16,24},{17,... | collective-permute-start | bytes 56 | tf_op jit(solution)/shard_map/ppermute | solution.py:476
  61.7 5.1 %collective-permute-done.13 = f32[2,2,1]{2,1,0:T(2,128)S(1)} collective-permute-done((f32[2,2,1]{2,1,0:T(2,128)S(1)}, f32[2,2,1]{2,1,0:T(2,128)S(1)}, u32[]{:S(2)}, u32[]{:S(2)}) %collective-permute-start.13) | collective-permute-done | bytes 48 | tf_op jit(solution)/shard_map/ppermute | solution.py:476
  66.8 0.7 copy.8
  (4 shorter events, 0.0 us)
Async XLA Ops:
  0.7 5.9 %copy-start.6 = (s32[1,4,6,2]{2,3,1,0:T(2,128)S(1)}, s32[1,4,6,2]{2,3,1,0:T(2,128)}, u32[]{:S(2)}) copy-start(s32[1,4,6,2]{2,3,1,0:T(2,128)} %param.10) | copy-start | bytes 580
  1.9 22.5 %collective-permute-start.4 = (bf16[2,6,2,128,128]{4,3,2,1,0:T(8,128)(2,1)S(1)}, bf16[2,6,2,128,128]{4,3,2,1,0:T(8,128)(2,1)S(1)}, u32[]{:S(2)}, u32[]{:S(2)}) collective-permute-start(bf16[2,6,2,128,128]{4,3,2,1,0:T(8,128)(2,1)S(1)} %pick_source.1.refs_9_.refs_10_), channel_id=1, source_target_pairs={{8,0},{10,2},{4,12},{6,14},{9,1},{11,3},{5,13},{7,15},{24,16},{26,... | collective-permute-start | bytes 2359304 | tf_op jit(solution)/shard_map/ppermute | solution.py:402
  6.5 2.2 %collective-permute-start.3 = (s32[1]{0:T(128)}, s32[1]{0:T(128)}, u32[]{:S(2)}, u32[]{:S(2)}) collective-permute-start(s32[1]{0:T(128)} %param.11), channel_id=1, source_target_pairs={{0,1},{1,0},{2,3},{3,2},{4,5},{5,4},{6,7},{7,6},{8,9},{9,8},{10,11... | collective-permute-start | bytes 20 | tf_op jit(solution)/shard_map/ppermute | solution.py:401
  6.8 23.8 %collective-permute-start.7 = (s32[48]{0:T(128)S(1)}, s32[48]{0:T(128)S(1)}, u32[]{:S(2)}, u32[]{:S(2)}) collective-permute-start(s32[48]{0:T(128)S(1)} %reshape.10.refs_5_.refs_7_), channel_id=1, source_target_pairs={{0,1},{1,0},{2,3},{3,2},{4,5},{5,4},{6,7},{7,6},{8,9},{9,8},{10,11... | collective-permute-start | bytes 584 | tf_op jit(solution)/shard_map/ppermute | solution.py:401
  7.3 17.1 %collective-permute-start.5 = (s32[48]{0:T(128)S(1)}, s32[48]{0:T(128)S(1)}, u32[]{:S(2)}, u32[]{:S(2)}) collective-permute-start(s32[48]{0:T(128)S(1)} %reshape.10.refs_5_.refs_7_), channel_id=1, source_target_pairs={{8,0},{10,2},{4,12},{6,14},{9,1},{11,3},{5,13},{7,15},{24,16},{26,... | collective-permute-start | bytes 584 | tf_op jit(solution)/shard_map/ppermute | solution.py:402
  8.6 30.0 %collective-permute-start.9 = (bf16[2,6,2,128,128]{4,3,2,1,0:T(8,128)(2,1)S(1)}, bf16[2,6,2,128,128]{4,3,2,1,0:T(8,128)(2,1)S(1)}, u32[]{:S(2)}, u32[]{:S(2)}) collective-permute-start(bf16[2,6,2,128,128]{4,3,2,1,0:T(8,128)(2,1)S(1)} %pick_source.1.refs_9_.refs_10_), channel_id=1, source_target_pairs={{0,1},{1,0},{2,3},{3,2},{4,5},{5,4},{6,7},{7,6},{8,9},{9,8},{10,11... | collective-permute-start | bytes 2359304 | tf_op jit(solution)/shard_map/ppermute | solution.py:401
  10.7 20.2 %copy-start.3 = (s32[4]{0:T(128)S(1)}, s32[4]{0:T(128)}, u32[]{:S(2)}) copy-start(s32[4]{0:T(128)} %get-tuple-element.63.order_ref.refs_0_) | copy-start | bytes 52
  10.7 20.2 %copy-start.5 = (s32[8]{0:T(128)S(1)}, s32[8]{0:T(128)}, u32[]{:S(2)}) copy-start(s32[8]{0:T(128)} %get-tuple-element.68.refs_1_) | copy-start | bytes 100
  14.2 32.9 %collective-permute-start.10 = (bf16[2,6,2,128,128]{4,3,2,1,0:T(8,128)(2,1)}, bf16[2,6,2,128,128]{4,3,2,1,0:T(8,128)(2,1)S(1)}, u32[]{:S(2)}, u32[]{:S(2)}) collective-permute-start(bf16[2,6,2,128,128]{4,3,2,1,0:T(8,128)(2,1)} %get-tuple-element.69.refs_11_), channel_id=1, source_target_pairs={{8,0},{10,2},{4,12},{6,14},{9,1},{11,3},{5,13},{7,15},{24,16},{26,... | collective-permute-start | bytes 2359304 | tf_op jit(solution)/shard_map/ppermute | solution.py:402
  24.4 14.2 %collective-permute-start.6 = (s32[48]{0:T(128)S(1)}, s32[48]{0:T(128)S(1)}, u32[]{:S(2)}, u32[]{:S(2)}) collective-permute-start(s32[48]{0:T(128)S(1)} %collective-permute-done.5.refs_4_.refs_6_), channel_id=1, source_target_pairs={{0,1},{1,0},{2,3},{3,2},{4,5},{5,4},{6,7},{7,6},{8,9},{9,8},{10,11... | collective-permute-start | bytes 584 | tf_op jit(solution)/shard_map/ppermute | solution.py:401
  24.4 32.6 %collective-permute-start.11 = (bf16[2,6,2,128,128]{4,3,2,1,0:T(8,128)(2,1)}, bf16[2,6,2,128,128]{4,3,2,1,0:T(8,128)(2,1)}, u32[]{:S(2)}, u32[]{:S(2)}) collective-permute-start(bf16[2,6,2,128,128]{4,3,2,1,0:T(8,128)(2,1)} %get-tuple-element.75.refs_12_), channel_id=1, source_target_pairs={{8,0},{10,2},{4,12},{6,14},{9,1},{11,3},{5,13},{7,15},{24,16},{26,... | collective-permute-start | bytes 2359304 | tf_op jit(solution)/shard_map/ppermute | solution.py:402
  30.6 8.0 %collective-permute-start.8 = (bf16[2,6,2,128,128]{4,3,2,1,0:T(8,128)(2,1)S(1)}, bf16[2,6,2,128,128]{4,3,2,1,0:T(8,128)(2,1)S(1)}, u32[]{:S(2)}, u32[]{:S(2)}) collective-permute-start(bf16[2,6,2,128,128]{4,3,2,1,0:T(8,128)(2,1)S(1)} %collective-permute-done.4.refs_8_.refs_0_), channel_id=1, source_target_pairs={{0,1},{1,0},{2,3},{3,2},{4,5},{5,4},{6,7},{7,6},{8,9},{9,8},{10,11... | collective-permute-start | bytes 2359304 | tf_op jit(solution)/shard_map/ppermute | solution.py:401
  30.9 1.1 %copy-start = (bf16[2,6,2,128,128]{4,3,2,1,0:T(8,128)(2,1)S(1)}, bf16[2,6,2,128,128]{4,3,2,1,0:T(8,128)(2,1)}, u32[]{:S(2)}) copy-start(bf16[2,6,2,128,128]{4,3,2,1,0:T(8,128)(2,1)} %get-tuple-element.75.refs_12_) | copy-start | bytes 2359300
  32.0 1.1 %copy-start.2 = (bf16[2,6,2,128,128]{4,3,2,1,0:T(8,128)(2,1)S(1)}, bf16[2,6,2,128,128]{4,3,2,1,0:T(8,128)(2,1)}, u32[]{:S(2)}) copy-start(bf16[2,6,2,128,128]{4,3,2,1,0:T(8,128)(2,1)} %get-tuple-element.69.refs_11_) | copy-start | bytes 2359300
  33.1 5.5 %copy-start.1 = (bf16[2,6,2,128,128]{4,3,2,1,0:T(8,128)(2,1)S(1)}, bf16[2,6,2,128,128]{4,3,2,1,0:T(8,128)(2,1)}, u32[]{:S(2)}) copy-start(bf16[2,6,2,128,128]{4,3,2,1,0:T(8,128)(2,1)} %get-tuple-element.75.refs_12_) | copy-start | bytes 2359300
  48.7 8.3 %copy-start.4 = (s32[8]{0:T(128)S(1)}, s32[8]{0:T(128)}, u32[]{:S(2)}) copy-start(s32[8]{0:T(128)} %get-tuple-element.64.sinks_ref) | copy-start | bytes 100
  59.2 1.2 %collective-permute-start.12 = (f32[2,2,1]{2,1,0:T(2,128)S(1)}, f32[2,2,1]{2,1,0:T(2,128)S(1)}, u32[]{:S(2)}, u32[]{:S(2)}) collective-permute-start(f32[2,2,1]{2,1,0:T(2,128)S(1)} %get-tuple-element.79), channel_id=1, source_target_pairs={{0,1},{1,0},{2,3},{3,2},{4,5},{5,4},{6,7},{7,6},{8,9},{9,8},{10,11... | collective-permute-start | bytes 56 | tf_op jit(solution)/shard_map/ppermute | solution.py:401
  60.4 6.4 %collective-permute-start.13 = (f32[2,2,1]{2,1,0:T(2,128)S(1)}, f32[2,2,1]{2,1,0:T(2,128)S(1)}, u32[]{:S(2)}, u32[]{:S(2)}) collective-permute-start(f32[2,2,1]{2,1,0:T(2,128)S(1)} %add.6), channel_id=1, source_target_pairs={{0,8},{1,9},{2,10},{3,11},{12,4},{13,5},{14,6},{15,7},{16,24},{17,... | collective-permute-start | bytes 56 | tf_op jit(solution)/shard_map/ppermute | solution.py:476
where the time goes:
time: 67.9 us; the launch traced here: 67.4 us
  Pallas kernels  24.7 us (36%)
  waiting for transfers between devices  22.4 us (33%)
  starting transfers between devices  15.7 us (23%)
  local copies, waits for them, and re-layouts  3.15 us (5%)
  between operations  1.43 us (2%)
    ppermute x4, waiting for transfers between devices, local(): to_partner = lambda value: lax.ppermute(value, 'mom', pairs)  16.2 us
    ppermute x4, starting transfers between devices, local(): to_partner = lambda value: lax.ppermute(value, 'mom', pairs)  13.4 us
    pallas_call x2, Pallas kernels, weights(): pl.pallas_call(lambda *refs: weights_kernel(s, *refs), out_shape=jax.Shap...  12.2 us
    ppermute x1, waiting for transfers between devices, local(): return total + lax.ppermute(total, both, back)  5.08 us
    pallas_call x1, Pallas kernels, pick_others(): pl.pallas_call(pick_kernel, out_shape=[jax.ShapeDtypeStruct(fields.shape[...  3.51 us
    pallas_call x2, Pallas kernels, inner(): pl.pallas_call(lambda *refs: inner_kernel(slot, *refs), out_shape=jax.Sha...  3.31 us
    unnamed x15, local copies, waits for them, and re-layouts  2.4 us
    pallas_call x1, Pallas kernels, last(): pl.pallas_call(last_kernel, out_shape=[jax.ShapeDtypeStruct((2, share, 1)...  2.14 us
  transfers between devices with their start and end apart: 11, of which 4 were waited for; matrix products, arithmetic and copies ran while one was open for 0% of the time, Pallas kernels for 32%

commit v1 on v0

--- a/solution.py
+++ b/solution.py
@@ -275,29 +275,17 @@
     )(order, active, far_time, own_time, far_cols, own_cols, m_cols, b_cols, a, d, *picked)
 
 
-def products(field_ref, u_refs, slot, held, sems):
+def products(field_ref, u_refs, slot):
     _, rows, per_row, size, _ = field_ref.shape
-    copies = [
-        [
-            pltpu.make_async_copy(field_ref.at[part, r], held.at[part, r], sems.at[part, r])
-            for part in range(2)
-        ]
-        for r in range(rows)
-    ]
-    for row in copies:
-        for copy in row:
-            copy.start()
     chunk = min(size, 32)
     fold = lambda x: jnp.sum(x.reshape(chunk // 8, 8, size), axis=0)
     sums = [jnp.zeros((8, size), F32) for _ in range(2 * len(u_refs))]
     for r in range(rows):
-        for copy in copies[r]:
-            copy.wait()
         for j in range(per_row):
             for start in range(0, size, chunk):
                 at = pl.ds(start, chunk)
-                real = held[0, r, j, at].astype(F32)
-                imag = held[1, r, j, at].astype(F32)
+                real = field_ref[0, r, j, at].astype(F32)
+                imag = field_ref[1, r, j, at].astype(F32)
                 for s, u_ref in enumerate(u_refs):
                     u_real, u_imag = u_ref[slot, r, j, 0, at], u_ref[slot, r, j, 1, at]
                     sums[2 * s] += fold(real * u_real - imag * u_imag)
@@ -305,12 +293,8 @@
     return sums
 
 
-def products_scratch(field):
-    return [pltpu.VMEM(field.shape, field.dtype), pltpu.SemaphoreType.DMA(field.shape[:2])]
-
-
-def inner_kernel(slot, field_ref, u0_ref, u1_ref, out_ref, held, sems):
-    for at, value in enumerate(products(field_ref, (u0_ref, u1_ref), slot, held, sems)):
+def inner_kernel(slot, field_ref, u0_ref, u1_ref, out_ref):
+    for at, value in enumerate(products(field_ref, (u0_ref, u1_ref), slot)):
         out_ref[at] = value
 
 
@@ -318,9 +302,8 @@
     return pl.pallas_call(
         lambda *refs: inner_kernel(slot, *refs),
         out_shape=jax.ShapeDtypeStruct((4, 8, field.shape[-1]), F32),
-        in_specs=[ANY, VMEM, VMEM],
+        in_specs=[VMEM] * 3,
         out_specs=VMEM,
-        scratch_shapes=products_scratch(field),
         cost_estimate=cost(4_000_000, 4_000_000),
         compiler_params=pltpu.CompilerParams(vmem_limit_bytes=24 * 2**20),
         name="inner",
@@ -354,13 +337,13 @@
 
 
 def last_kernel(core_ref, order_ref, sinks_ref, *refs):
-    *others, field_ref, u0_ref, u1_ref, mine_ref, theirs_ref, held, sems = refs
+    *others, field_ref, u0_ref, u1_ref, mine_ref, theirs_ref = refs
     slots = order_ref.shape[0]
     deltas = sinks_ref.shape[0] // 2
     share = deltas // 2
     core = core_ref[0]
     sums = [[ref[at] for at in range(4)] for ref in others]
-    sums.insert(slots - 2, products(field_ref, (u0_ref, u1_ref), 0, held, sems))
+    sums.insert(slots - 2, products(field_ref, (u0_ref, u1_ref), 0))
     for out_ref, owner in ((mine_ref, core), (theirs_ref, 1 - core)):
         lines = [jnp.zeros(sums[0][0].shape, F32) for _ in range(2 * share)]
         for slot in range(slots):
@@ -382,9 +365,8 @@
     return pl.pallas_call(
         last_kernel,
         out_shape=[jax.ShapeDtypeStruct((2, share, 1), F32)] * 2,
-        in_specs=[SMEM] * 3 + [VMEM] * len(others) + [ANY, VMEM, VMEM],
+        in_specs=[SMEM] * 3 + [VMEM] * (len(others) + 3),
         out_specs=[VMEM] * 2,
-        scratch_shapes=products_scratch(field),
         cost_estimate=cost(4_000_000, 4_000_000),
         compiler_params=pltpu.CompilerParams(vmem_limit_bytes=24 * 2**20),
         name="last",

time: 67.9 us -> 76.4 us (1.13)
  waiting for transfers between devices: 22.4 us -> 32.3 us
  Pallas kernels: 24.7 us -> 21 us
  starting transfers between devices: 15.7 us -> 17.9 us
    ppermute x0 -> x1, waiting for transfers between devices: none -> 17.8 us  [branch(): field = lax.ppermute(field, both, routes)]
    ppermute x4, waiting for transfers between devices: 16.2 us -> 8.31 us  [local(): to_partner = lambda value: lax.ppermute(value, 'mom', pairs)]
    ppermute x0 -> x1, starting transfers between devices: none -> 2.34 us  [branch(): field = lax.ppermute(field, both, routes)]
    pallas_call x2, Pallas kernels: 12.2 us -> 10.4 us  [weights(): pl.pallas_call(lambda *refs: weights_kernel(s, *refs), out_shape=jax.Shap...]
    pallas_call x2 -> x3, Pallas kernels: 3.31 us -> 1.84 us  [inner(): pl.pallas_call(lambda *refs: inner_kernel(slot, *refs), out_shape=jax.Sha...]
  transfers between devices with their start and end apart: 11 -> 12, of which waited for: 4 -> 4; matrix products, arithmetic and copies ran while one was open for 0% -> 0% of each run, Pallas kernels for 32% -> 24%
where the time goes in v1:
time: 76.4 us; the launch traced here: 75.9 us
  waiting for transfers between devices  32.3 us (42%)
  Pallas kernels  21 us (27%)
  starting transfers between devices  17.9 us (23%)
  local copies, waits for them, and re-layouts  3.15 us (4%)
  between operations  1.42 us (2%)
    ppermute x1, waiting for transfers between devices, branch(): field = lax.ppermute(field, both, routes)  17.8 us
    ppermute x4, starting transfers between devices, local(): to_partner = lambda value: lax.ppermute(value, 'mom', pairs)  13.4 us
    pallas_call x2, Pallas kernels, weights(): pl.pallas_call(lambda *refs: weights_kernel(s, *refs), out_shape=jax.Shap...  10.4 us
    ppermute x4, waiting for transfers between devices, local(): to_partner = lambda value: lax.ppermute(value, 'mom', pairs)  8.31 us
    ppermute x1, waiting for transfers between devices, local(): return total + lax.ppermute(total, both, back)  5.08 us
    pallas_call x1, Pallas kernels, pick_others(): pl.pallas_call(pick_kernel, out_shape=[jax.ShapeDtypeStruct(fields.shape[...  3.51 us
    unnamed x15, local copies, waits for them, and re-layouts  2.4 us
    ppermute x1, starting transfers between devices, branch(): field = lax.ppermute(field, both, routes)  2.34 us
  transfers between devices with their start and end apart: 12, of which 4 were waited for; matrix products, arithmetic and copies ran while one was open for 0% of the time, Pallas kernels for 24%

profile of v1, /device:TPU:8, one launch (start us, length us, event | category | flops | bytes accessed | tf_op | source)
XLA Modules:
  0.0 75.9 jit_solution(11731221684566416740)
XLA Ops:
  0.7 0.0 copy-start.6
  0.7 1.3 %pick_source.1.refs_9_.refs_10_ = bf16[2,6,2,128,128]{4,3,2,1,0:T(8,128)(2,1)S(1)} custom-call(s32[1]{0:T(128)S(6)} %copy.21.own_ref.source_ref.refs_2_.refs_3_, bf16[4,2,6,2,128,128]{5,4,3,2,1,0:T(8,128)(2,1)} %bitcast.3), custom_call_target="tpu_custom_call" | custom-call | bytes 1600000 | tf_op jit(solution)/shard_map/pick_source/pallas_call | solution.py:40
  1.9 4.5 %collective-permute-start.4 = (bf16[2,6,2,128,128]{4,3,2,1,0:T(8,128)(2,1)S(1)}, bf16[2,6,2,128,128]{4,3,2,1,0:T(8,128)(2,1)S(1)}, u32[]{:S(2)}, u32[]{:S(2)}) collective-permute-start(bf16[2,6,2,128,128]{4,3,2,1,0:T(8,128)(2,1)S(1)} %pick_source.1.refs_9_.refs_10_), channel_id=1, source_target_pairs={{8,0},{10,2},{4,12},{6,14},{9,1},{11,3},{5,13},{7,15},{24,16},{26,... | collective-permute-start | bytes 2359304 | tf_op jit(solution)/shard_map/ppermute | solution.py:384
  6.5 0.1 collective-permute-start.3
  6.6 0.0 copy-done.6
  6.6 0.1 copy.7
  6.7 0.1 reshape.10.refs_5_.refs_7_
  6.8 0.6 collective-permute-start.7
  7.3 1.3 %collective-permute-start.5 = (s32[48]{0:T(128)S(1)}, s32[48]{0:T(128)S(1)}, u32[]{:S(2)}, u32[]{:S(2)}) collective-permute-start(s32[48]{0:T(128)S(1)} %reshape.10.refs_5_.refs_7_), channel_id=1, source_target_pairs={{8,0},{10,2},{4,12},{6,14},{9,1},{11,3},{5,13},{7,15},{24,16},{26,... | collective-permute-start | bytes 584 | tf_op jit(solution)/shard_map/ppermute | solution.py:384
  8.6 0.1 collective-permute-start.9
  8.7 0.0 collective-permute-done.3.other_ref.refs_2_.refs_3_
  8.7 1.9 %plan.1 = (s32[4]{0:T(128)}, s32[8]{0:T(128)}, s32[8]{0:T(128)}, s32[1]{0:T(128)}) custom-call(s32[1]{0:T(128)} %bitcast.core_ref, s32[1]{0:T(128)S(6)} %copy.21.own_ref.source_ref.refs_2_.refs_3_, s32[1]{0:T(128)} %collective-permute-done.3.other_ref.refs_2_.refs_3_, s32[4]{0:T(128)} %deltas_ref.1), custom_call_target="tpu_custom_call" | custom-call | bytes 1000 | tf_op jit(solution)/shard_map/plan/pallas_call | solution.py:121
  10.7 0.0 copy-start.3
  10.7 0.0 copy-start.5
  10.7 3.5 %pick_others.1 = (bf16[2,6,2,128,128]{4,3,2,1,0:T(8,128)(2,1)}, bf16[2,6,2,128,128]{4,3,2,1,0:T(8,128)(2,1)}, bf16[2,6,2,128,128]{4,3,2,1,0:T(8,128)(2,1)S(1)}) custom-call(s32[4]{0:T(128)} %get-tuple-element.63.order_ref.refs_0_, bf16[4,2,6,2,128,128]{5,4,3,2,1,0:T(8,128)(2,1)} %bitcast.4), custom_call_target="tpu_custom_call" | custom-call | bytes 4800000 | tf_op jit(solution)/shard_map/pick_others/pallas_call | solution.py:67
  14.2 1.3 %collective-permute-start.10 = (bf16[2,6,2,128,128]{4,3,2,1,0:T(8,128)(2,1)}, bf16[2,6,2,128,128]{4,3,2,1,0:T(8,128)(2,1)S(1)}, u32[]{:S(2)}, u32[]{:S(2)}) collective-permute-start(bf16[2,6,2,128,128]{4,3,2,1,0:T(8,128)(2,1)} %get-tuple-element.69.refs_11_), channel_id=1, source_target_pairs={{8,0},{10,2},{4,12},{6,14},{9,1},{11,3},{5,13},{7,15},{24,16},{26,... | collective-permute-start | bytes 2359304 | tf_op jit(solution)/shard_map/ppermute | solution.py:384
  16.1 8.3 %collective-permute-done.5.refs_4_.refs_6_ = s32[48]{0:T(128)S(1)} collective-permute-done((s32[48]{0:T(128)S(1)}, s32[48]{0:T(128)S(1)}, u32[]{:S(2)}, u32[]{:S(2)}) %collective-permute-start.5) | collective-permute-done | bytes 224 | tf_op jit(solution)/shard_map/ppermute | solution.py:384
  24.4 0.0 collective-permute-start.6
  24.4 0.0 collective-permute-done.4.refs_8_.refs_0_
  24.4 6.2 %collective-permute-start.11 = (bf16[2,6,2,128,128]{4,3,2,1,0:T(8,128)(2,1)}, bf16[2,6,2,128,128]{4,3,2,1,0:T(8,128)(2,1)}, u32[]{:S(2)}, u32[]{:S(2)}) collective-permute-start(bf16[2,6,2,128,128]{4,3,2,1,0:T(8,128)(2,1)} %get-tuple-element.75.refs_12_), channel_id=1, source_target_pairs={{8,0},{10,2},{4,12},{6,14},{9,1},{11,3},{5,13},{7,15},{24,16},{26,... | collective-permute-start | bytes 2359304 | tf_op jit(solution)/shard_map/ppermute | solution.py:384
  30.6 0.0 collective-permute-done.7.refs_5_
  30.6 0.2 collective-permute-start.8
  30.9 0.0 copy-done.3
  30.9 0.0 copy-done.5
  30.9 1.1 %copy-done = bf16[2,6,2,128,128]{4,3,2,1,0:T(8,128)(2,1)S(1)} copy-done((bf16[2,6,2,128,128]{4,3,2,1,0:T(8,128)(2,1)S(1)}, bf16[2,6,2,128,128]{4,3,2,1,0:T(8,128)(2,1)}, u32[]{:S(2)}) %copy-start) | copy-done | bytes 786456
  32.0 1.1 %copy-done.2 = bf16[2,6,2,128,128]{4,3,2,1,0:T(8,128)(2,1)S(1)} copy-done((bf16[2,6,2,128,128]{4,3,2,1,0:T(8,128)(2,1)S(1)}, bf16[2,6,2,128,128]{4,3,2,1,0:T(8,128)(2,1)}, u32[]{:S(2)}) %copy-start.2) | copy-done | bytes 786456
  33.1 5.5 %weights.2.refs_1_ = f32[4,6,2,2,128,128]{5,4,3,2,1,0:T(8,128)S(1)} custom-call(s32[4]{0:T(128)S(1)} %copy-done.3, s32[8]{0:T(128)S(1)} %copy-done.5, s32[1]{0:T(128)S(6)} %copy.21.own_ref.source_ref.refs_2_.refs_3_, s32[1]{0:T(128)S(6)} %copy.21.own_ref.source_ref.refs_2_.refs_3_, s32[48]{0:T(128)S(1)} %collective-permute-done.5.refs_4_.refs_6_, ...), custom_call_target="tpu_custom_call" | custom-call | flops 80000000000 | bytes 4000000 | tf_op jit(solution)/shard_map/weights/pallas_call | solution.py:249
  38.6 0.0 collective-permute-done.6.refs_4_
  38.6 0.0 collective-permute-done.9.refs_9_
  38.6 0.0 collective-permute-done.8.refs_8_
  38.7 0.0 copy-done.1
  38.7 4.9 %weights.3.refs_2_ = f32[4,6,2,2,128,128]{5,4,3,2,1,0:T(8,128)S(1)} custom-call(s32[4]{0:T(128)S(1)} %copy-done.3, s32[8]{0:T(128)S(1)} %copy-done.5, s32[1]{0:T(128)} %collective-permute-done.3.other_ref.refs_2_.refs_3_, s32[1]{0:T(128)} %collective-permute-done.3.other_ref.refs_2_.refs_3_, s32[48]{0:T(128)S(1)} %collective-permute-done.6.refs_4_, ...), custom_call_target="tpu_custom_call" | custom-call | flops 2000000000 | bytes 4000000 | tf_op jit(solution)/shard_map/weights/pallas_call | solution.py:249
  43.6 0.6 inner.8.refs_0_
  44.2 0.0 collective-permute-done.10.refs_0_
  44.2 0.6 inner.9.refs_1_
  44.8 0.0 copy-start.4
  44.8 21.1 %conditional.1 = (f32[4,8,128]{2,1,0:T(8,128)S(1)}, f32[1,6,2,2,128,128]{5,4,3,2,1,0:T(8,128)S(1)}, f32[1,6,2,2,128,128]{5,4,3,2,1,0:T(8,128)S(1)}) conditional(s32[]{:T(128)} %bitcast.2, (f32[4,6,2,2,128,128]{5,4,3,2,1,0:T(8,128)S(1)}, f32[4,6,2,2,128,128]{5,4,3,2,1,0:T(8,128)S(1)}) %tuple.25, ...), branch_computations={%region_0.0_spmd, %region_1.0_spmd, %region_2.0_spmd, %region_3.0_... | conditional | flops 4000000 | bytes 13145792 | solution.py:453
  44.9 2.3 %collective-permute-start = (bf16[2,6,2,128,128]{4,3,2,1,0:T(8,128)(2,1)S(1)}, bf16[2,6,2,128,128]{4,3,2,1,0:T(8,128)(2,1)S(1)}, u32[]{:S(2)}, u32[]{:S(2)}) collective-permute-start(bf16[2,6,2,128,128]{4,3,2,1,0:T(8,128)(2,1)S(1)} %get-tuple-element.31), channel_id=1, source_target_pairs={{8,0},{10,2},{4,12},{6,14},{24,16},{26,18},{20,28},{22,30}} | collective-permute-start | bytes 2359304 | tf_op jit(solution)/shard_map/cond/branch_1_fun/ppermute | solution.py:443
  47.2 0.3 stage.5
  47.6 17.8 %collective-permute-done.refs_0_ = bf16[2,6,2,128,128]{4,3,2,1,0:T(8,128)(2,1)S(1)} collective-permute-done((bf16[2,6,2,128,128]{4,3,2,1,0:T(8,128)(2,1)S(1)}, bf16[2,6,2,128,128]{4,3,2,1,0:T(8,128)(2,1)S(1)}, u32[]{:S(2)}, u32[]{:S(2)}) %collective-permute-start) | collective-permute-done | bytes 786464 | tf_op jit(solution)/shard_map/cond/branch_1_fun/ppermute | solution.py:443
  65.4 0.6 inner.5
  66.0 0.0 collective-permute-done.11.refs_3_
  66.0 1.7 %last.1 = (f32[2,2,1]{2,1,0:T(2,128)S(1)}, f32[2,2,1]{2,1,0:T(2,128)S(1)}) custom-call(s32[1]{0:T(128)} %bitcast.core_ref, s32[4]{0:T(128)S(1)} %copy-done.3, s32[8]{0:T(128)S(1)} %copy-done.4, f32[4,8,128]{2,1,0:T(8,128)S(1)} %inner.8.refs_0_, f32[4,8,128]{2,1,0:T(8,128)S(1)} %inner.9.refs_1_, f32[4,8,128]{2,1,0:T(8,128)S(1)} %get-tuple-element.74.refs_2_, ...), custom_call_target="tpu_custom_call" | custom-call | flops 4000000 | bytes 4000000 | tf_op jit(solution)/shard_map/last/pallas_call | solution.py:365
  67.7 0.0 collective-permute-start.12
  67.7 1.1 %collective-permute-done.12 = f32[2,2,1]{2,1,0:T(2,128)S(1)} collective-permute-done((f32[2,2,1]{2,1,0:T(2,128)S(1)}, f32[2,2,1]{2,1,0:T(2,128)S(1)}, u32[]{:S(2)}, u32[]{:S(2)}) %collective-permute-start.12) | collective-permute-done | bytes 48 | tf_op jit(solution)/shard_map/ppermute | solution.py:383
  68.9 1.3 %collective-permute-start.13 = (f32[2,2,1]{2,1,0:T(2,128)S(1)}, f32[2,2,1]{2,1,0:T(2,128)S(1)}, u32[]{:S(2)}, u32[]{:S(2)}) collective-permute-start(f32[2,2,1]{2,1,0:T(2,128)S(1)} %add.6), channel_id=1, source_target_pairs={{0,8},{1,9},{2,10},{3,11},{12,4},{13,5},{14,6},{15,7},{16,24},{17,... | collective-permute-start | bytes 56 | tf_op jit(solution)/shard_map/ppermute | solution.py:458
  70.2 5.1 %collective-permute-done.13 = f32[2,2,1]{2,1,0:T(2,128)S(1)} collective-permute-done((f32[2,2,1]{2,1,0:T(2,128)S(1)}, f32[2,2,1]{2,1,0:T(2,128)S(1)}, u32[]{:S(2)}, u32[]{:S(2)}) %collective-permute-start.13) | collective-permute-done | bytes 48 | tf_op jit(solution)/shard_map/ppermute | solution.py:458
  75.3 0.7 copy.8
  (6 shorter events, 0.0 us)
Async XLA Ops:
  0.7 5.9 %copy-start.6 = (s32[1,4,6,2]{2,3,1,0:T(2,128)S(1)}, s32[1,4,6,2]{2,3,1,0:T(2,128)}, u32[]{:S(2)}) copy-start(s32[1,4,6,2]{2,3,1,0:T(2,128)} %param.10) | copy-start | bytes 580
  1.9 22.5 %collective-permute-start.4 = (bf16[2,6,2,128,128]{4,3,2,1,0:T(8,128)(2,1)S(1)}, bf16[2,6,2,128,128]{4,3,2,1,0:T(8,128)(2,1)S(1)}, u32[]{:S(2)}, u32[]{:S(2)}) collective-permute-start(bf16[2,6,2,128,128]{4,3,2,1,0:T(8,128)(2,1)S(1)} %pick_source.1.refs_9_.refs_10_), channel_id=1, source_target_pairs={{8,0},{10,2},{4,12},{6,14},{9,1},{11,3},{5,13},{7,15},{24,16},{26,... | collective-permute-start | bytes 2359304 | tf_op jit(solution)/shard_map/ppermute | solution.py:384
  6.5 2.2 %collective-permute-start.3 = (s32[1]{0:T(128)}, s32[1]{0:T(128)}, u32[]{:S(2)}, u32[]{:S(2)}) collective-permute-start(s32[1]{0:T(128)} %param.11), channel_id=1, source_target_pairs={{0,1},{1,0},{2,3},{3,2},{4,5},{5,4},{6,7},{7,6},{8,9},{9,8},{10,11... | collective-permute-start | bytes 20 | tf_op jit(solution)/shard_map/ppermute | solution.py:383
  6.8 23.8 %collective-permute-start.7 = (s32[48]{0:T(128)S(1)}, s32[48]{0:T(128)S(1)}, u32[]{:S(2)}, u32[]{:S(2)}) collective-permute-start(s32[48]{0:T(128)S(1)} %reshape.10.refs_5_.refs_7_), channel_id=1, source_target_pairs={{0,1},{1,0},{2,3},{3,2},{4,5},{5,4},{6,7},{7,6},{8,9},{9,8},{10,11... | collective-permute-start | bytes 584 | tf_op jit(solution)/shard_map/ppermute | solution.py:383
  7.3 17.1 %collective-permute-start.5 = (s32[48]{0:T(128)S(1)}, s32[48]{0:T(128)S(1)}, u32[]{:S(2)}, u32[]{:S(2)}) collective-permute-start(s32[48]{0:T(128)S(1)} %reshape.10.refs_5_.refs_7_), channel_id=1, source_target_pairs={{8,0},{10,2},{4,12},{6,14},{9,1},{11,3},{5,13},{7,15},{24,16},{26,... | collective-permute-start | bytes 584 | tf_op jit(solution)/shard_map/ppermute | solution.py:384
  8.6 30.0 %collective-permute-start.9 = (bf16[2,6,2,128,128]{4,3,2,1,0:T(8,128)(2,1)S(1)}, bf16[2,6,2,128,128]{4,3,2,1,0:T(8,128)(2,1)S(1)}, u32[]{:S(2)}, u32[]{:S(2)}) collective-permute-start(bf16[2,6,2,128,128]{4,3,2,1,0:T(8,128)(2,1)S(1)} %pick_source.1.refs_9_.refs_10_), channel_id=1, source_target_pairs={{0,1},{1,0},{2,3},{3,2},{4,5},{5,4},{6,7},{7,6},{8,9},{9,8},{10,11... | collective-permute-start | bytes 2359304 | tf_op jit(solution)/shard_map/ppermute | solution.py:383
  10.7 20.2 %copy-start.3 = (s32[4]{0:T(128)S(1)}, s32[4]{0:T(128)}, u32[]{:S(2)}) copy-start(s32[4]{0:T(128)} %get-tuple-element.63.order_ref.refs_0_) | copy-start | bytes 52
  10.7 20.2 %copy-start.5 = (s32[8]{0:T(128)S(1)}, s32[8]{0:T(128)}, u32[]{:S(2)}) copy-start(s32[8]{0:T(128)} %get-tuple-element.68.refs_1_) | copy-start | bytes 100
  14.2 30.0 %collective-permute-start.10 = (bf16[2,6,2,128,128]{4,3,2,1,0:T(8,128)(2,1)}, bf16[2,6,2,128,128]{4,3,2,1,0:T(8,128)(2,1)S(1)}, u32[]{:S(2)}, u32[]{:S(2)}) collective-permute-start(bf16[2,6,2,128,128]{4,3,2,1,0:T(8,128)(2,1)} %get-tuple-element.69.refs_11_), channel_id=1, source_target_pairs={{8,0},{10,2},{4,12},{6,14},{9,1},{11,3},{5,13},{7,15},{24,16},{26,... | collective-permute-start | bytes 2359304 | tf_op jit(solution)/shard_map/ppermute | solution.py:384
  24.4 14.2 %collective-permute-start.6 = (s32[48]{0:T(128)S(1)}, s32[48]{0:T(128)S(1)}, u32[]{:S(2)}, u32[]{:S(2)}) collective-permute-start(s32[48]{0:T(128)S(1)} %collective-permute-done.5.refs_4_.refs_6_), channel_id=1, source_target_pairs={{0,1},{1,0},{2,3},{3,2},{4,5},{5,4},{6,7},{7,6},{8,9},{9,8},{10,11... | collective-permute-start | bytes 584 | tf_op jit(solution)/shard_map/ppermute | solution.py:383
  24.4 41.6 %collective-permute-start.11 = (bf16[2,6,2,128,128]{4,3,2,1,0:T(8,128)(2,1)}, bf16[2,6,2,128,128]{4,3,2,1,0:T(8,128)(2,1)}, u32[]{:S(2)}, u32[]{:S(2)}) collective-permute-start(bf16[2,6,2,128,128]{4,3,2,1,0:T(8,128)(2,1)} %get-tuple-element.75.refs_12_), channel_id=1, source_target_pairs={{8,0},{10,2},{4,12},{6,14},{9,1},{11,3},{5,13},{7,15},{24,16},{26,... | collective-permute-start | bytes 2359304 | tf_op jit(solution)/shard_map/ppermute | solution.py:384
  30.6 8.0 %collective-permute-start.8 = (bf16[2,6,2,128,128]{4,3,2,1,0:T(8,128)(2,1)S(1)}, bf16[2,6,2,128,128]{4,3,2,1,0:T(8,128)(2,1)S(1)}, u32[]{:S(2)}, u32[]{:S(2)}) collective-permute-start(bf16[2,6,2,128,128]{4,3,2,1,0:T(8,128)(2,1)S(1)} %collective-permute-done.4.refs_8_.refs_0_), channel_id=1, source_target_pairs={{0,1},{1,0},{2,3},{3,2},{4,5},{5,4},{6,7},{7,6},{8,9},{9,8},{10,11... | collective-permute-start | bytes 2359304 | tf_op jit(solution)/shard_map/ppermute | solution.py:383
  30.9 1.1 %copy-start = (bf16[2,6,2,128,128]{4,3,2,1,0:T(8,128)(2,1)S(1)}, bf16[2,6,2,128,128]{4,3,2,1,0:T(8,128)(2,1)}, u32[]{:S(2)}) copy-start(bf16[2,6,2,128,128]{4,3,2,1,0:T(8,128)(2,1)} %get-tuple-element.75.refs_12_) | copy-start | bytes 2359300
  32.0 1.1 %copy-start.2 = (bf16[2,6,2,128,128]{4,3,2,1,0:T(8,128)(2,1)S(1)}, bf16[2,6,2,128,128]{4,3,2,1,0:T(8,128)(2,1)}, u32[]{:S(2)}) copy-start(bf16[2,6,2,128,128]{4,3,2,1,0:T(8,128)(2,1)} %get-tuple-element.69.refs_11_) | copy-start | bytes 2359300
  33.1 5.5 %copy-start.1 = (bf16[2,6,2,128,128]{4,3,2,1,0:T(8,128)(2,1)S(1)}, bf16[2,6,2,128,128]{4,3,2,1,0:T(8,128)(2,1)}, u32[]{:S(2)}) copy-start(bf16[2,6,2,128,128]{4,3,2,1,0:T(8,128)(2,1)} %get-tuple-element.75.refs_12_) | copy-start | bytes 2359300
  44.8 21.2 %copy-start.4 = (s32[8]{0:T(128)S(1)}, s32[8]{0:T(128)}, u32[]{:S(2)}) copy-start(s32[8]{0:T(128)} %get-tuple-element.64.sinks_ref) | copy-start | bytes 100
  44.9 20.5 %collective-permute-start = (bf16[2,6,2,128,128]{4,3,2,1,0:T(8,128)(2,1)S(1)}, bf16[2,6,2,128,128]{4,3,2,1,0:T(8,128)(2,1)S(1)}, u32[]{:S(2)}, u32[]{:S(2)}) collective-permute-start(bf16[2,6,2,128,128]{4,3,2,1,0:T(8,128)(2,1)S(1)} %get-tuple-element.31), channel_id=1, source_target_pairs={{8,0},{10,2},{4,12},{6,14},{24,16},{26,18},{20,28},{22,30}} | collective-permute-start | bytes 2359304 | tf_op jit(solution)/shard_map/cond/branch_1_fun/ppermute | solution.py:443
  67.7 1.2 %collective-permute-start.12 = (f32[2,2,1]{2,1,0:T(2,128)S(1)}, f32[2,2,1]{2,1,0:T(2,128)S(1)}, u32[]{:S(2)}, u32[]{:S(2)}) collective-permute-start(f32[2,2,1]{2,1,0:T(2,128)S(1)} %get-tuple-element.79), channel_id=1, source_target_pairs={{0,1},{1,0},{2,3},{3,2},{4,5},{5,4},{6,7},{7,6},{8,9},{9,8},{10,11... | collective-permute-start | bytes 56 | tf_op jit(solution)/shard_map/ppermute | solution.py:383
  68.9 6.4 %collective-permute-start.13 = (f32[2,2,1]{2,1,0:T(2,128)S(1)}, f32[2,2,1]{2,1,0:T(2,128)S(1)}, u32[]{:S(2)}, u32[]{:S(2)}) collective-permute-start(f32[2,2,1]{2,1,0:T(2,128)S(1)} %add.6), channel_id=1, source_target_pairs={{0,8},{1,9},{2,10},{3,11},{12,4},{13,5},{14,6},{15,7},{16,24},{17,... | collective-permute-start | bytes 56 | tf_op jit(solution)/shard_map/ppermute | solution.py:458
